TPU v7x, 128 devices: a whole 4x4x4 slice. The times are simulated.
128 devices in a mesh: row: 16 (over x, y_lo, core), col: 8 (over y_hi, z).
Axes of the slice: x: 4, y: 4 (y_hi: 2, y_lo: 2; y = y_hi * 2 + y_lo), z: 4, core: 2. Of those that a mesh axis runs over, the one named last changes fastest.
Arguments:
- front_init: float32 [16384, 16384], P('row', 'col'), as said below
- child_tiles: bfloat16 [4096, 256, 256], P(('row', 'col'))
- child_dest: int32 [4096], P(('row', 'col')), may hold values from 0 to 4095, as said below
Outputs:
- panel_factor: float32 [16384, 1024], P('row')
- schur_update: float32 [16384, 16384], P('row', 'col')
Inputs may be any that keep to these rules, and one draw needn't show every extreme that they name: `child_dest`: t = 64 * tile row + tile column. A tile held at col index c has its tile column in c * 8 to (c + 1) * 8 - 1. Of one device's tiles at most 4 have tile rows in one block of 4 tile rows, and in every column of the mesh one such block gets exactly 4 from every device of that column. The leading 1024 x 1024 block of front_init plus any child tiles added to it is strictly diagonally dominant.
All inputs are finite; a program needn't handle non-finite values.
Results may differ from a plain program's by a relative error of at most 0.0003.
Values may be sent and summed in bfloat16 or wider, within the bound.
A program may use at most 192 MiB of HBM per device.

v0:
```python
import jax
import jax.numpy as jnp
from jax import lax
from jax.sharding import PartitionSpec as P

PW = 1024
CAP = 4


def broadcast(array, axis, root):
    mine = lax.axis_index(axis) == root
    return lax.psum(jnp.where(mine, array, jnp.zeros_like(array)), axis)


def body(front_init, child_tiles, child_dest):
    row_count = lax.axis_size("row")
    col_count = lax.axis_size("col")
    row_extent, col_extent = front_init.shape
    tile_width = child_tiles.shape[1]
    tile_grid = col_extent * col_count // tile_width
    row_tiles = row_extent // tile_width
    col_tiles = col_extent // tile_width
    capacity = CAP
    tile_count = child_tiles.shape[0]
    col_index = lax.axis_index("col")
    tile_row = child_dest // tile_grid
    tile_col = child_dest % tile_grid
    owner_row = tile_row // row_tiles
    local_tile = (tile_row - owner_row * row_tiles) * col_tiles + (tile_col - col_index * col_tiles)
    same_owner = owner_row[:, None] == owner_row[None, :]
    positions = jnp.arange(tile_count)
    earlier = positions[None, :] < positions[:, None]
    send_rank = jnp.sum((same_owner & earlier).astype(jnp.int32), axis=1)
    send_slot = owner_row * capacity + send_rank
    outgoing = (
        jnp.zeros((row_count * capacity, tile_width, tile_width), jnp.bfloat16)
        .at[send_slot]
        .set(child_tiles)
    )
    targets = jnp.full((row_count * capacity,), -1, jnp.int32).at[send_slot].set(local_tile)
    arrived, places = (
        lax.all_to_all(outgoing, "row", split_axis=0, concat_axis=0, tiled=True),
        lax.all_to_all(targets, "row", split_axis=0, concat_axis=0, tiled=True),
    )
    onehot = (places[None, :] == jnp.arange(row_tiles * col_tiles)[:, None]).astype(jnp.bfloat16)
    summed = jnp.dot(
        onehot,
        arrived.reshape(arrived.shape[0], tile_width * tile_width),
        preferred_element_type=jnp.float32,
    )
    added_tiles = (
        summed.reshape(row_tiles, col_tiles, tile_width, tile_width)
        .transpose(0, 2, 1, 3)
        .reshape(row_extent, col_extent)
    )
    front_sum = front_init + added_tiles
    column_panel = broadcast(front_sum[:, :PW], "col", 0)
    pivot_raw = broadcast(column_panel, "row", 0)
    pivot_sym = (pivot_raw + pivot_raw.T) * 0.5
    pivot_factor = jnp.linalg.cholesky(pivot_sym)
    row_factor = jax.scipy.linalg.solve_triangular(pivot_factor, column_panel.T, lower=True).T
    group_size = row_count // col_count
    pieces = []
    for offset in range(group_size):
        pieces.append(broadcast(row_factor, "row", group_size * col_index + offset))
    strip_factor = jnp.concatenate(pieces, axis=0)
    schur_update = front_sum - jnp.dot(
        row_factor,
        strip_factor.T,
        precision=lax.Precision.HIGHEST,
        preferred_element_type=jnp.float32,
    )
    return (row_factor, schur_update)


def solution(mesh):
    return jax.shard_map(
        body,
        mesh=mesh,
        in_specs=(P("row", "col"), P(("row", "col"), None, None), P(("row", "col"))),
        out_specs=(P("row", None), P("row", "col")),
        check_vma=False,
    )
```

profile of v0, /device:TPU:5, one launch (start us, length us, event | category | flops | bytes accessed | tf_op | source)
XLA Modules:
  0.0 1077.5 jit_solution(15334882516940550699)
XLA Ops:
  9.4 6.1 all-to-all-start
  15.6 4.2 broadcast_in_dim.9
  19.8 11.3 %scatter_fusion = bf16[64,256,256]{2,1,0:T(8,128)(2,1)} fusion(bf16[64,256,256]{2,1,0:T(8,128)(2,1)} %broadcast_in_dim.9, s32[32]{0:T(128)S(1)} %compare_select_fusion, bf16[32,256,256]{2,1,0:T(8,128)(2,1)} %param.4), kind=kCustom, calls=%fused_computation.1 | custom fusion | bytes 12583040 | tf_op jit(solution)/shard_map/scatter | solution.py:38
  31.1 5.7 all-to-all-start.1
  36.9 9.3 copy.80
  47.4 108.8 %all-to-all-done.1 = bf16[64,256,256]{2,1,0:T(8,128)(2,1)} async-done(((bf16[64,256,256]{2,1,0:T(8,128)(2,1)}), bf16[64,256,256]{2,1,0:T(8,128)(2,1)}, u32[]{:S(2)}, u32[]{:S(2)}) %all-to-all-start.1) | async-done | bytes 8388640 | tf_op jit(solution)/shard_map/all_to_all | solution.py:42
  156.3 9.4 fusion
  165.7 7.3 copy.114
  173.0 9.3 copy.110
  182.3 12.1 %add.120 = f32[1024,2048]{0,1:T(8,128)} add(f32[1024,2048]{0,1:T(8,128)} %copy.80, f32[1024,2048]{0,1:T(8,128)} %copy.110) | non-fusion elementwise | flops 2097152 | bytes 25165824 | tf_op jit(solution)/shard_map/add | solution.py:56
  194.5 5.0 slice_select_fusion
  199.6 125.8 %all-reduce.6.cloned.1.call-done = f32[1024,1024]{0,1:T(8,128)} async-done(((f32[1024,1024]{0,1:T(8,128)}), f32[1024,1024]{0,1:T(8,128)}) %all-reduce.6.cloned.1.call-update) | async-done | bytes 4194320 | tf_op jit(solution)/shard_map/psum | solution.py:12
  325.4 2.8 broadcast_select_fusion.2
  328.3 122.2 %all-reduce.8.cloned.1.call-done = f32[1024,1024]{0,1:T(8,128)} async-done(((f32[1024,1024]{0,1:T(8,128)}), f32[1024,1024]{0,1:T(8,128)}) %all-reduce.8.cloned.1.call-update) | async-done | bytes 4194320 | tf_op jit(solution)/shard_map/psum | solution.py:12
  450.6 5.3 copy.81
  455.9 6.9 fusion.7
  462.8 13.8 %copy.82 = f32[1024,1024]{0,1:T(8,128)} copy(f32[1024,1024]{1,0:T(8,128)} %fusion.7) | data formatting | bytes 8388608 | tf_op jit(solution)/shard_map/mul | solution.py:59
  476.6 4.4 fusion.6
  481.1 2.0 copy-done.3
  483.1 11.7 %cholesky.222 = f32[128,128]{1,0:T(8,128)S(1)} custom-call(f32[128,128]{1,0:T(8,128)S(1)} %cholesky.577), custom_call_target="Cholesky" | custom-call | tf_op jit(solution)/shard_map/jit(cholesky)/cholesky | solution.py:60
  494.9 9.8 custom-call.63
  508.1 11.7 %cholesky.243 = f32[128,128]{1,0:T(8,128)S(1)} custom-call(f32[128,128]{1,0:T(8,128)S(1)} %cholesky.581), custom_call_target="Cholesky" | custom-call | tf_op jit(solution)/shard_map/jit(cholesky)/cholesky | solution.py:60
  520.1 9.8 custom-call.64
  531.1 2.0 copy-done
  533.0 2.4 convolution_subtract_fusion.6
  535.5 11.7 %cholesky.466 = f32[128,128]{1,0:T(8,128)S(1)} custom-call(f32[128,128]{1,0:T(8,128)S(1)} %cholesky.586), custom_call_target="Cholesky" | custom-call | tf_op jit(solution)/shard_map/jit(cholesky)/cholesky | solution.py:60
  548.0 9.8 custom-call.65
  559.0 3.5 convolution_subtract_fusion.7
  562.6 11.7 %cholesky.485 = f32[128,128]{1,0:T(8,128)S(1)} custom-call(f32[128,128]{1,0:T(8,128)S(1)} %cholesky.591), custom_call_target="Cholesky" | custom-call | tf_op jit(solution)/shard_map/jit(cholesky)/cholesky | solution.py:60
  575.1 9.8 custom-call.66
  586.0 3.2 convolution_subtract_fusion.8
  589.2 11.9 %cholesky.504 = f32[128,128]{1,0:T(8,128)S(1)} custom-call(f32[128,128]{1,0:T(8,128)S(1)} %cholesky.596), custom_call_target="Cholesky" | custom-call | tf_op jit(solution)/shard_map/jit(cholesky)/cholesky | solution.py:60
  601.8 9.8 custom-call.67
  612.7 3.1 convolution_subtract_fusion.9
  615.8 11.7 %cholesky.524 = f32[128,128]{1,0:T(8,128)S(1)} custom-call(f32[128,128]{1,0:T(8,128)S(1)} %cholesky.601), custom_call_target="Cholesky" | custom-call | tf_op jit(solution)/shard_map/jit(cholesky)/cholesky | solution.py:60
  628.3 9.8 custom-call.68
  639.1 3.1 convolution_subtract_fusion.10
  642.2 11.7 %cholesky.544 = f32[128,128]{1,0:T(8,128)S(1)} custom-call(f32[128,128]{1,0:T(8,128)S(1)} %cholesky.606), custom_call_target="Cholesky" | custom-call | tf_op jit(solution)/shard_map/jit(cholesky)/cholesky | solution.py:60
  654.7 9.8 custom-call.69
  665.4 2.1 convolution_subtract_fusion.11
  667.5 11.7 %cholesky.562 = f32[128,128]{1,0:T(8,128)S(1)} custom-call(f32[128,128]{1,0:T(8,128)S(1)} %convolution_subtract_fusion.11), custom_call_target="Cholesky" | custom-call | tf_op jit(solution)/shard_map/jit(cholesky)/cholesky | solution.py:60
  689.4 4.9 select_select_fusion
  694.3 23.7 %while.1 = (s32[]{:T(128)}, f32[1024,1024]{0,1:T(8,128)}, s32[8,2]{0,1:T(2,128)S(1)}, f32[8,128,128]{2,1,0:T(8,128)S(1)}, s32[]{:T(128)}) while((s32[]{:T(128)}, f32[1024,1024]{0,1:T(8,128)}, s32[8,2]{0,1:T(2,128)S(1)}, f32[8,128,128]{2,1,0:T(8,128)S(1)}, s32[]{:T(128)}) %tuple.63), condition=%wide.while_cond, body=%wide.while_body.sunk | while | flops 2 | bytes 393329 | solution.py:61
  695.0 2.2 dynamic-slice.7
  697.9 2.2 dynamic-slice.7
  700.9 2.2 dynamic-slice.7
  703.9 2.2 dynamic-slice.7
  706.9 2.2 dynamic-slice.7
  709.8 2.2 dynamic-slice.7
  712.8 2.2 dynamic-slice.7
  715.8 2.2 dynamic-slice.7
  718.1 78.8 %custom-call.70 = f32[8,128,128]{1,2,0:T(8,128)S(1)} custom-call(f32[8,128,128]{2,1,0:T(8,128)S(1)} %get-tuple-element.9), custom_call_target="InvertDiagBlocksLowerTriangular" | custom-call | tf_op jit(solution)/shard_map/jit(_solve_triangular)/triangular_solve | solution.py:61
  796.9 1.9 constant_dynamic-update-slice_fusion.17
  798.8 1.7 convolution_subtract_fusion.4
  803.7 2.0 fusion.25
  806.5 2.2 fusion.28
  809.4 2.6 convolution_subtract_fusion.2
  812.7 2.9 convolution_subtract_fusion.1
  816.2 3.5 convolution_subtract_fusion.3
  820.4 4.5 broadcast_select_fusion
  824.9 5.3 copy.100
  830.2 198.7 %all-reduce.10.cloned.1.call-done = (f32[1024,1024]{0,1:T(8,128)}, f32[1024,1024]{0,1:T(8,128)}) async-done(((f32[1024,1024]{0,1:T(8,128)}, f32[1024,1024]{0,1:T(8,128)}), (f32[1024,1024]{0,1:T(8,128)}, f32[1024,1024]{0,1:T(8,128)})) %all-reduce.10.cloned.1.call-update) | async-done | bytes 8388624 | tf_op jit(solution)/shard_map/psum | solution.py:12
  1028.9 32.6 %fusion.8 = f32[1024,2048]{0,1:T(8,128)} fusion(f32[1024,2048]{0,1:T(8,128)} %add.120, f32[1024,1024]{1,0:T(8,128)} %copy-done.1, f32[1024,1024]{0,1:T(8,128)} %get-tuple-element.42, f32[1024,1024]{0,1:T(8,128)} %get-tuple-element.43), kind=kOutput, calls=%fused_computation.18 | convolution fusion | flops 25773998080 | bytes 29360128 | tf_op jit(solution)/shard_map/dot_general | solution.py:67
  1061.5 9.1 copy.101
  (113 shorter events, 35.4 us)
Async XLA Ops:
  9.4 21.7 %all-to-all-start = ((s32[16,4,1]{1,2,0:T(1,128)}), s32[16,4,1]{1,2,0:T(1,128)S(1)}, u32[]{:S(2)}, u32[]{:S(2)}) async-start(s32[16,4,1]{1,2,0:T(1,128)} %bitcast), calls=%async_computation | async-start | bytes 16384 | tf_op jit(solution)/shard_map/all_to_all | solution.py:43
  31.1 125.2 %all-to-all-start.1 = ((bf16[64,256,256]{2,1,0:T(8,128)(2,1)}), bf16[64,256,256]{2,1,0:T(8,128)(2,1)}, u32[]{:S(2)}, u32[]{:S(2)}) async-start(bf16[64,256,256]{2,1,0:T(8,128)(2,1)} %scatter_fusion), calls=%async_computation.1 | async-start | bytes 16777216 | tf_op jit(solution)/shard_map/all_to_all | solution.py:42
  36.8 288.6 %all-reduce.6.cloned.1.call-start = ((), (), s32[]{:S(2)}) async-start(), calls=%async_computation.2 | async-start | bytes 8388608 | tf_op jit(solution)/shard_map/psum | solution.py:12
  199.5 251.0 %all-reduce.8.cloned.1.call-start = ((), (), s32[]{:S(2)}) async-start(), calls=%async_computation.3 | async-start | bytes 8388608 | tf_op jit(solution)/shard_map/psum | solution.py:12
  328.3 700.6 %all-reduce.10.cloned.1.call-start = ((), (), s32[]{:S(2)}) async-start(), calls=%async_computation.4 | async-start | bytes 16777216 | tf_op jit(solution)/shard_map/psum | solution.py:12
  481.1 2.0 copy-start.3
  531.1 2.0 copy-start
  796.9 4.4 copy-start.2
  820.4 4.5 copy-start.1
Sparse Core Ops, SparseCore 0:
  199.6 125.7 all-reduce.5
  328.5 122.0 all-reduce.7
  825.0 203.8 all-reduce.9
where the time goes:
time: 1090 us; the launch traced here: 1080 us
  waiting for transfers between devices  556 us (51%)
  other arithmetic  289 us (27%)
  local copies, waits for them, and re-layouts  110 us (10%)
  matrix products  91.7 us (8%)
  between operations  19.5 us (2%)
  starting transfers between devices  12 us (1%)
    psum x3, waiting for transfers between devices, broadcast(): return lax.psum(jnp.where(mine, array, jnp.zeros_like(array)), axis)  447 us
    another operation x30, other arithmetic, body(): pivot_factor = jnp.linalg.cholesky(pivot_sym)  168 us
    all_to_all x1, waiting for transfers between devices, body(): lax.all_to_all(outgoing, 'row', split_axis=0, concat_axis=0, tiled=True)  109 us
    another operation x3, other arithmetic, body(): jax.scipy.linalg.solve_triangular(pivot_factor, column_panel.T, lower=True)  83.7 us
    unnamed x12, local copies, waits for them, and re-layouts  35 us
    dot_general x1, matrix products, body(): jnp.dot(row_factor, strip_factor.T, precision=lax.Precision.HIGHEST, pref...  32.6 us
    another operation x14, matrix products, body(): pivot_factor = jnp.linalg.cholesky(pivot_sym)  26.3 us
    another operation x40, local copies, waits for them, and re-layouts  23.5 us
  transfers between devices with their start and end apart: 5, of which 4 were waited for; matrix products, arithmetic and copies ran while one was open for 3% of the time, Pallas kernels for 0%

commit v1 on v0

--- a/solution.py
+++ b/solution.py
@@ -9,7 +9,7 @@
 
 def broadcast(array, axis, root):
     mine = lax.axis_index(axis) == root
-    return lax.psum(jnp.where(mine, array, jnp.zeros_like(array)), axis)
+    return jnp.sum(lax.all_gather(jnp.where(mine, array, jnp.zeros_like(array)), axis), axis=0)
 
 
 def body(front_init, child_tiles, child_dest):

time: 1090 us -> 2030 us (1.86)
  waiting for transfers between devices: 556 us -> 1430 us
  other arithmetic: 289 us -> 373 us
  local copies, waits for them, and re-layouts: 110 us -> 66.8 us
  matrix products: 91.7 us -> 119 us
    all_gather x0 -> x4, waiting for transfers between devices: none -> 1310 us  [broadcast(): lax.all_gather(jnp.where(mine, array, jnp.zeros_like(array)), axis)]
    psum x3 -> x0, waiting for transfers between devices: 447 us -> none  [broadcast(): return lax.psum(jnp.where(mine, array, jnp.zeros_like(array)), axis)]
    reduce_sum x0 -> x4, other arithmetic: none -> 86.3 us  [broadcast(): jnp.sum(lax.all_gather(jnp.where(mine, array, jnp.zeros_like(array)), axi...]
    another operation x15, matrix products: 23.4 us -> 54 us  [body(): jax.scipy.linalg.solve_triangular(pivot_factor, column_panel.T, lower=True)]
    unnamed x12 -> x24, local copies, waits for them, and re-layouts: 35 us -> 11.5 us
  transfers between devices with their start and end apart: 5 -> 6, of which waited for: 4 -> 5; matrix products, arithmetic and copies ran while one was open for 3% -> 2% of each run, Pallas kernels for 0% -> 0%
where the time goes in v1:
time: 2030 us; the launch traced here: 2020 us
  waiting for transfers between devices  1430 us (70%)
  other arithmetic  373 us (18%)
  matrix products  119 us (6%)
  local copies, waits for them, and re-layouts  66.8 us (3%)
    all_gather x4, waiting for transfers between devices, broadcast(): lax.all_gather(jnp.where(mine, array, jnp.zeros_like(array)), axis)  1310 us
    another operation x30, other arithmetic, body(): pivot_factor = jnp.linalg.cholesky(pivot_sym)  172 us
    all_to_all x1, waiting for transfers between devices, body(): lax.all_to_all(outgoing, 'row', split_axis=0, concat_axis=0, tiled=True)  118 us
    reduce_sum x4, other arithmetic, broadcast(): jnp.sum(lax.all_gather(jnp.where(mine, array, jnp.zeros_like(array)), axi...  86.3 us
    another operation x3, other arithmetic, body(): jax.scipy.linalg.solve_triangular(pivot_factor, column_panel.T, lower=True)  83.8 us
    another operation x15, matrix products, body(): jax.scipy.linalg.solve_triangular(pivot_factor, column_panel.T, lower=True)  54 us
  transfers between devices with their start and end apart: 6, of which 5 were waited for; matrix products, arithmetic and copies ran while one was open for 2% of the time, Pallas kernels for 0%

profile of v1, /device:TPU:5, one launch (start us, length us, event | category | flops | bytes accessed | tf_op | source)
XLA Modules:
  0.0 2018.5 jit_solution(15326442308682413248)
XLA Ops:
  9.4 6.1 all-to-all-start
  15.6 4.4 broadcast_in_dim.9
  20.0 11.2 scatter_fusion
  31.2 5.7 all-to-all-start.1
  38.3 118.1 %all-to-all-done.1 = bf16[64,256,256]{2,1,0:T(8,128)(2,1)} async-done(((bf16[64,256,256]{2,1,0:T(8,128)(2,1)}), bf16[64,256,256]{2,1,0:T(8,128)(2,1)}, u32[]{:S(2)}, u32[]{:S(2)}) %all-to-all-start.1) | async-done | bytes 8388640 | tf_op jit(solution)/shard_map/all_to_all | solution.py:42
  156.3 9.4 fusion
  165.8 7.5 copy.71
  173.3 11.9 add.112
  185.2 5.0 slice_select_fusion
  190.3 349.5 %all-gather.9.cloned.1.call-done = f32[8192,1024]{1,0:T(8,128)} async-done(((f32[1024,1024]{1,0:T(8,128)}), f32[8192,1024]{1,0:T(8,128)}) %all-gather.9.cloned.1.call-update) | async-done | bytes 33554448 | tf_op jit(solution)/shard_map/all_gather | solution.py:12
  539.8 14.7 reduce_sum.46
  554.5 2.8 broadcast_select_fusion.2
  557.4 326.3 %all-gather.11.cloned.1.call-done = f32[16384,1024]{1,0:T(8,128)} async-done(((f32[1024,1024]{1,0:T(8,128)}), f32[16384,1024]{1,0:T(8,128)}) %all-gather.11.cloned.1.call-update) | async-done | bytes 67108880 | tf_op jit(solution)/shard_map/all_gather | solution.py:12
  883.7 22.9 %reduce_sum.47 = f32[1024,1024]{1,0:T(8,128)} reduce(f32[16,1024,1024]{2,1,0:T(8,128)} %bitcast.7, f32[]{:T(128)} %constant.332.clone.1), dimensions={0}, to_apply=%region_4.5 | reduce | flops 15728640 | bytes 71303168 | tf_op jit(solution)/shard_map/reduce_sum | solution.py:12
  906.6 5.5 copy.44
  912.2 4.5 fusion.7
  918.5 11.7 cholesky.222
  930.3 2.5 cholesky.254
  932.8 9.8 custom-call.63
  942.6 2.4 constant_dynamic-update-slice_fusion.32
  946.6 11.9 cholesky.243
  959.1 9.8 custom-call.64
  972.3 11.7 cholesky.466
  985.2 9.8 custom-call.65
  996.2 2.3 convolution_subtract_fusion.7
  998.6 12.1 cholesky.485
  1012.0 9.8 custom-call.66
  1022.9 2.3 convolution_subtract_fusion.8
  1025.2 11.7 cholesky.504
  1038.2 10.0 custom-call.67
  1049.2 2.3 convolution_subtract_fusion.9
  1051.5 11.7 cholesky.524
  1064.5 9.8 custom-call.68
  1077.3 11.9 cholesky.544
  1090.5 9.8 custom-call.69
  1102.9 11.7 cholesky.562
  1121.4 4.8 select_select_fusion
  1126.2 22.8 %while.1 = (s32[]{:T(128)}, f32[1024,1024]{1,0:T(8,128)}, s32[8,2]{0,1:T(2,128)S(1)}, f32[8,128,128]{2,1,0:T(8,128)S(1)}, s32[]{:T(128)}) while((s32[]{:T(128)}, f32[1024,1024]{1,0:T(8,128)}, s32[8,2]{0,1:T(2,128)S(1)}, f32[8,128,128]{2,1,0:T(8,128)S(1)}, s32[]{:T(128)}) %tuple.59), condition=%wide.while_cond, body=%wide.while_body.sunk | while | flops 2 | bytes 131189 | solution.py:61
  1126.9 2.2 bitcast_dynamic-update-slice_fusion.2
  1129.7 2.2 bitcast_dynamic-update-slice_fusion.2
  1132.6 2.2 bitcast_dynamic-update-slice_fusion.2
  1135.5 2.2 bitcast_dynamic-update-slice_fusion.2
  1138.3 2.2 bitcast_dynamic-update-slice_fusion.2
  1141.2 2.2 bitcast_dynamic-update-slice_fusion.2
  1144.1 2.2 bitcast_dynamic-update-slice_fusion.2
  1146.9 2.2 bitcast_dynamic-update-slice_fusion.2
  1149.1 79.0 %custom-call.70 = f32[8,128,128]{1,2,0:T(8,128)S(1)} custom-call(f32[8,128,128]{2,1,0:T(8,128)S(1)} %get-tuple-element.9), custom_call_target="InvertDiagBlocksLowerTriangular" | custom-call | tf_op jit(solution)/shard_map/jit(_solve_triangular)/triangular_solve | solution.py:61
  1228.1 3.1 constant_dynamic-update-slice_fusion.17
  1235.5 2.9 convolution_subtract_fusion
  1240.6 3.8 fusion.25
  1244.4 2.8 constant_dynamic-update-slice_fusion.14
  1248.0 5.4 fusion.28
  1254.7 3.3 constant_dynamic-update-slice_fusion.13
  1258.0 6.3 convolution_subtract_fusion.2
  1264.3 2.7 constant_dynamic-update-slice_fusion.12
  1267.0 7.3 convolution_subtract_fusion.1
  1275.8 7.5 convolution_subtract_fusion.3
  1284.4 2.1 copy.57
  1291.3 4.6 broadcast_select_fusion
  1296.5 328.9 %all-gather.13.cloned.1.call-done = f32[16384,1024]{1,0:T(8,128)} async-done(((f32[1024,1024]{1,0:T(8,128)}), f32[16384,1024]{1,0:T(8,128)}) %all-gather.13.cloned.1.call-update) | async-done | bytes 67108880 | tf_op jit(solution)/shard_map/all_gather | solution.py:12
  1625.3 25.7 %reduce_sum.48 = f32[1024,1024]{1,0:T(8,128)} reduce(f32[16,1024,1024]{2,1,0:T(8,128)} %bitcast.33, f32[]{:T(128)} %constant.332.clone.1), dimensions={0}, to_apply=%region_21.22 | reduce | flops 15728640 | bytes 71303168 | tf_op jit(solution)/shard_map/reduce_sum | solution.py:12
  1651.1 305.2 %all-gather.15.cloned.1.call-done = f32[16384,1024]{1,0:T(8,128)} async-done(((f32[1024,1024]{1,0:T(8,128)}), f32[16384,1024]{1,0:T(8,128)}) %all-gather.15.cloned.1.call-update) | async-done | bytes 67108880 | tf_op jit(solution)/shard_map/all_gather | solution.py:12
  1956.2 22.9 %reduce_sum.49 = f32[1024,1024]{1,0:T(8,128)} reduce(f32[16,1024,1024]{2,1,0:T(8,128)} %bitcast.34, f32[]{:T(128)} %constant.332.clone.1), dimensions={0}, to_apply=%region_22.23 | reduce | flops 15728640 | bytes 71303168 | tf_op jit(solution)/shard_map/reduce_sum | solution.py:12
  1979.2 32.4 %fusion.8 = f32[1024,2048]{1,0:T(8,128)} fusion(f32[1024,2048]{1,0:T(8,128)} %add.112, f32[1024,1024]{0,1:T(8,128)} %copy-done.1, f32[1024,1024]{1,0:T(8,128)} %reduce_sum.49, f32[1024,1024]{1,0:T(8,128)} %reduce_sum.48), kind=kOutput, calls=%fused_computation.17 | convolution fusion | flops 25773998080 | bytes 29360128 | tf_op jit(solution)/shard_map/dot_general | solution.py:67
  (103 shorter events, 49.7 us)
Async XLA Ops:
  9.4 21.8 %all-to-all-start = ((s32[16,4,1]{1,2,0:T(1,128)}), s32[16,4,1]{1,2,0:T(1,128)S(1)}, u32[]{:S(2)}, u32[]{:S(2)}) async-start(s32[16,4,1]{1,2,0:T(1,128)} %bitcast), calls=%async_computation | async-start | bytes 16384 | tf_op jit(solution)/shard_map/all_to_all | solution.py:43
  31.2 125.2 %all-to-all-start.1 = ((bf16[64,256,256]{2,1,0:T(8,128)(2,1)}), bf16[64,256,256]{2,1,0:T(8,128)(2,1)}, u32[]{:S(2)}, u32[]{:S(2)}) async-start(bf16[64,256,256]{2,1,0:T(8,128)(2,1)} %scatter_fusion), calls=%async_computation.1 | async-start | bytes 16777216 | tf_op jit(solution)/shard_map/all_to_all | solution.py:42
  36.9 502.9 %all-gather.9.cloned.1.call-start = ((), (), s32[]{:S(2)}) async-start(), calls=%async_computation.2 | async-start | bytes 37748736 | tf_op jit(solution)/shard_map/all_gather | solution.py:12
  190.2 693.5 %all-gather.11.cloned.1.call-start = ((), (), s32[]{:S(2)}) async-start(), calls=%async_computation.3 | async-start | bytes 71303168 | tf_op jit(solution)/shard_map/all_gather | solution.py:12
  557.3 1068.0 %all-gather.13.cloned.1.call-start = ((), (), s32[]{:S(2)}) async-start(), calls=%async_computation.4 | async-start | bytes 71303168 | tf_op jit(solution)/shard_map/all_gather | solution.py:12
  916.6 1.9 copy-start
  1228.1 10.4 copy-start.7
  1247.2 0.8 copy-start.6
  1267.0 7.3 copy-start.2
  1284.4 5.4 copy-start.3
  1288.5 1.0 copy-start.5
  1288.5 1.2 copy-start.4
  1291.3 4.6 copy-start.1
  1295.9 660.4 %all-gather.15.cloned.1.call-start = ((), (), s32[]{:S(2)}) async-start(), calls=%async_computation.5 | async-start | bytes 71303168 | tf_op jit(solution)/shard_map/all_gather | solution.py:12
Sparse Core Ops, SparseCore 0:
  190.3 349.4 all-gather.8
  557.4 326.2 all-gather.10
  1296.0 329.2 all-gather.12
  1626.9 329.2 all-gather.14
